TPU v7x, 32 devices: a whole 2x2x4 slice. The times are simulated.
32 devices in a mesh: pipe: 2 (over core), dp: 16 (over z, y, x).
Axes of the slice: x: 2, y: 2, z: 4, core: 2. Of those that a mesh axis runs over, the one named last changes fastest.
Arguments:
- gate: bfloat16 [2, 1, 2048, 4096], P('pipe', None, 'dp'), may hold values from -5 to 5
- filters: bfloat16 [2, 256, 128], P('pipe', 'dp'), may hold values from -0.75 to 0.75
- doc_ids: int32 [1, 2048], P(None, 'dp'), may hold values from 0 to 1, as said below
- loss_grad: bfloat16 [1, 2048, 4096], P(None, 'dp'), may hold values from -6 to 6
Outputs:
- input_grads: bfloat16 [2, 1, 2048, 4096], P('pipe', None, 'dp')
Inputs may be any that keep to these rules, and one draw needn't show every extreme that they name: `doc_ids`: within each window the ids never fall, begin at 0 and end at 1, and every document holds 128 or more tokens.
All inputs are finite; a program needn't handle non-finite values.
Results may differ from a plain program's by a relative error of at most 0.0049.
Values may be sent and summed in bfloat16 or wider, within the bound.
A program may use at most 64 MiB of HBM per device.

v0:
```python
import jax
import jax.numpy as jnp
from jax import lax
from jax.sharding import PartitionSpec as P


def passed_along(value, axis, by):
    count = lax.axis_size(axis)
    pairs = [(i, i + by) for i in range(count) if 0 <= i + by < count]
    return lax.ppermute(value, axis, pairs)


def band_table(filt_block, tap_count):
    groups = filt_block.shape[0]
    span_cols = 2 * tap_count
    base_row = jnp.concatenate(
        [filt_block, jnp.zeros((groups, span_cols + 1 - tap_count), filt_block.dtype)], axis=1
    )
    tiled_rows = jnp.broadcast_to(base_row[:, None, :], (groups, tap_count, span_cols + 1))
    tiled_rows = tiled_rows.reshape(groups, tap_count * (span_cols + 1))
    return tiled_rows[:, : tap_count * span_cols].reshape(groups, tap_count, span_cols)


def adjoint_block(filt_all, scaled_own, scaled_head, parity_own, parity_head):
    row_count, channels = scaled_own.shape
    groups, tap_count = filt_all.shape
    lane_width = channels // groups
    group_block = 64
    block_count = groups // group_block
    row_blocks = row_count // tap_count
    window = jnp.concatenate([scaled_own, scaled_head], axis=0)
    window_parity = jnp.concatenate([parity_own, parity_head], axis=0)
    arranged = window.reshape(
        row_count + tap_count, block_count, group_block, lane_width
    ).transpose(1, 0, 2, 3)
    front_rows = arranged[:, :row_count].reshape(
        block_count, row_blocks, tap_count, group_block, lane_width
    )
    behind = arranged[:, tap_count:].reshape(
        block_count, row_blocks, tap_count, group_block, lane_width
    )
    slabs = jnp.concatenate([front_rows, behind], axis=2)
    column_parity = jnp.concatenate(
        [
            window_parity[:row_count].reshape(row_blocks, tap_count),
            window_parity[tap_count:].reshape(row_blocks, tap_count),
        ],
        axis=1,
    )
    same_doc = parity_own.reshape(row_blocks, tap_count)[:, :, None] == column_parity[:, None, :]
    filt_blocks = filt_all.reshape(block_count, group_block, tap_count)

    def one_block(inputs):
        filt_part, slab_piece = inputs
        band_rows = band_table(filt_part, tap_count)
        masked = jnp.where(same_doc[:, None], band_rows[None], jnp.zeros((), band_rows.dtype))
        return jnp.einsum("rgtj,rjgc->rtgc", masked, slab_piece, preferred_element_type=jnp.float32)

    product = lax.map(one_block, (filt_blocks, slabs))
    return product.transpose(1, 2, 0, 3, 4).reshape(row_count, channels)


def body(gate, filters, doc_ids, loss_grad):
    gate_local = gate[0]
    micro_count, row_count, channels = gate_local.shape
    filt_all = lax.all_gather(filters, "dp", axis=1, tiled=True)[0]
    tap_count = filt_all.shape[1]
    section_count = lax.axis_size("pipe")
    section_index = lax.axis_index("pipe")
    parity = doc_ids % 2
    tick_count = micro_count + section_count - 1
    is_last = section_index == section_count - 1
    is_first = section_index == 0

    def one_tick(tick, carry):
        payload, results = carry
        received = passed_along(payload, "pipe", -1)
        micro_index = tick - (section_count - 1 - section_index)
        active = jnp.logical_and(micro_index >= 0, micro_index < micro_count)
        chosen = jnp.clip(micro_index, 0, micro_count - 1)
        own_loss = lax.dynamic_index_in_dim(loss_grad, chosen, 0, keepdims=False)
        incoming = jnp.where(is_last, own_loss, received)
        gate_now = lax.dynamic_index_in_dim(gate_local, chosen, 0, keepdims=False)
        parity_now = lax.dynamic_index_in_dim(parity, chosen, 0, keepdims=False)
        scaled = (gate_now.astype(jnp.float32) * incoming.astype(jnp.float32)).astype(jnp.bfloat16)
        scaled_head, parity_head = passed_along((scaled, parity_now), "dp", -1)

        def working(unused):
            update = adjoint_block(filt_all, scaled, scaled_head, parity_now, parity_head)
            return (incoming.astype(jnp.float32) + update).astype(jnp.bfloat16)

        def waiting(unused):
            return jnp.zeros_like(incoming)

        produced = lax.cond(active, working, waiting, 0)
        previous = lax.dynamic_index_in_dim(results, chosen, 0, keepdims=False)
        results = lax.dynamic_update_index_in_dim(
            results, jnp.where(active, produced, previous), chosen, 0
        )
        following = jnp.clip(tick + 1, 0, micro_count - 1)
        next_loss = lax.dynamic_index_in_dim(loss_grad, following, 0, keepdims=False)
        payload = jnp.where(is_first, next_loss, produced)
        return (payload, results)

    start_payload = jnp.where(is_first, loss_grad[0], jnp.zeros_like(loss_grad[0]))
    start_results = jnp.zeros_like(gate_local)
    _, results = lax.fori_loop(0, tick_count, one_tick, (start_payload, start_results))
    return results[None]


def solution(mesh):
    return jax.shard_map(
        body,
        mesh=mesh,
        in_specs=(
            P("pipe", None, "dp", None),
            P("pipe", "dp", None),
            P(None, "dp"),
            P(None, "dp", None),
        ),
        out_specs=P("pipe", None, "dp", None),
        check_vma=False,
    )
```

profile of v0, /device:TPU:0, one launch (start us, length us, event | category | flops | bytes accessed | tf_op | source)
XLA Modules:
  0.0 292.6 jit_solution(9645054348732942074)
XLA Ops:
  0.0 0.7 fusion.11
  0.7 1.3 collective-permute-start.2
  2.0 0.7 and_select_fusion
  2.6 1.7 copy.11
  4.3 1.0 select_bitcast_fusion
  5.4 43.9 %all_gather.3 = bf16[1,256,128]{2,1,0:T(8,128)(2,1)S(1)} all-gather(bf16[1,16,128]{2,1,0:T(8,128)(2,1)S(1)} %copy-done.1), channel_id=1, replica_groups=mesh['pipe'=2,'dp'=16] {'dp'}, dimensions={1}, use_global_device_ids=true | all-gather | bytes 69632 | tf_op jit(solution)/shard_map/all_gather | solution.py:66
  49.2 1.3 copy.12
  50.6 1.1 broadcast.71
  51.7 238.6 %while.28 = (s32[]{:T(128)}, bf16[128,4096]{0,1:T(8,128)(2,1)}, bf16[1,128,4096]{1,2,0:T(8,128)(2,1)}, pred[]{:T(512)}, bf16[1,128,4096]{1,2,0:T(8,128)(2,1)S(1)...) while((s32[]{:T(128)}, bf16[128,4096]{0,1:T(8,128)(2,1)}, ...), condition=%wide.region_5.6_spmd, body=%wide.region_0.5_spmd.sunk | while | flops 82870536 | bytes 83072224 | solution.py:107
  51.7 1.3 collective-permute-start
  53.0 3.5 %collective-permute-done = bf16[128,4096]{0,1:T(8,128)(2,1)S(1)} collective-permute-done((bf16[128,4096]{0,1:T(8,128)(2,1)}, bf16[128,4096]{0,1:T(8,128)(2,1)S(1)}, u32[]{:S(2)}, u32[]{:S(2)}) %collective-permute-start) | collective-permute-done | bytes 1048608 | tf_op jit(solution)/shard_map/while/body/eval_jaxpr/ppermute | solution.py:10
  56.5 2.7 fusion.17
  59.1 1.3 collective-permute-start.1
  60.4 25.8 %collective-permute-done.1 = bf16[128,4096]{0,1:T(8,128)(2,1)S(1)} collective-permute-done((bf16[128,4096]{0,1:T(8,128)(2,1)S(1)}, bf16[128,4096]{0,1:T(8,128)(2,1)S(1)}, u32[]{:S(2)}, u32[]{:S(2)}) %collective-permute-start.1) | collective-permute-done | bytes 1048608 | tf_op jit(solution)/shard_map/while/body/eval_jaxpr/ppermute | solution.py:10
  86.4 2.7 fusion.18
  89.1 1.3 collective-permute-start
  90.4 84.5 %collective-permute-done = bf16[128,4096]{0,1:T(8,128)(2,1)S(1)} collective-permute-done((bf16[128,4096]{0,1:T(8,128)(2,1)}, bf16[128,4096]{0,1:T(8,128)(2,1)S(1)}, u32[]{:S(2)}, u32[]{:S(2)}) %collective-permute-start) | collective-permute-done | bytes 1048608 | tf_op jit(solution)/shard_map/while/body/eval_jaxpr/ppermute | solution.py:10
  174.9 2.7 fusion.17
  177.5 1.3 collective-permute-start.1
  178.8 25.8 %collective-permute-done.1 = bf16[128,4096]{0,1:T(8,128)(2,1)S(1)} collective-permute-done((bf16[128,4096]{0,1:T(8,128)(2,1)S(1)}, bf16[128,4096]{0,1:T(8,128)(2,1)S(1)}, u32[]{:S(2)}, u32[]{:S(2)}) %collective-permute-start.1) | collective-permute-done | bytes 1048608 | tf_op jit(solution)/shard_map/while/body/eval_jaxpr/ppermute | solution.py:10
  204.6 83.0 %conditional.2 = (bf16[128,4096]{0,1:T(8,128)(2,1)S(1)}) conditional(s32[]{:T(128)} %convert_element_type.55, () %tuple.66, (bf16[128,4096]{0,1:T(8,128)(2,1)}, bf16[1,256,128]{2,1,0:T(8,128)(2,1)S(1)}, bf16[128,4096]{0,1:T(8,128)(2,1)S(1)}, bf16[128,4096]{0,1:T(8,128)(2,1)S(1)}, s32[1,128]{1,0:T(1,128)S(1)}, /*index=5*/s32[128]{0:T(128)S(1)}) %tuple.67), branch_computations={%region_1.1_spmd, %region_2.4_spmd} | conditional | flops 79200512 | bytes 64197568 | solution.py:95
  205.5 80.0 %while.27 = (s32[]{:T(128)}, f32[4,1,128,64,16]{2,4,3,1,0:T(8,128)}, bf16[4,1,256,64,16]{2,4,3,1,0:T(8,128)(2,1)S(1)}, bf16[4,64,128]{2,1,0:T(8,128)(2,1)S(1)}, ...) while((s32[]{:T(128)}, f32[4,1,128,64,16]{2,4,3,1,0:T(8,128)}, ...), condition=%wide.region_4.3_spmd.clone, body=%wide.region_3.2_spmd.clone.sunk | while | flops 69238784 | bytes 47418224 | solution.py:59
  205.6 3.2 %broadcast_in_dim.53 = bf16[64,128,257]{2,1,0:T(8,128)(2,1)} broadcast(bf16[64,257]{1,0:T(8,128)(2,1)S(1)} %concatenate.14), dimensions={0,2} | broadcast | bytes 4243584 | tf_op jit(solution)/shard_map/while/body/eval_jaxpr/cond/branch_1_fun/while/body/eval_jaxpr/broadcast_in_dim | solution.py:19
  208.8 10.8 %reshape.107 = bf16[64,32896]{1,0:T(8,128)(2,1)} reshape(bf16[64,128,257]{2,1,0:T(8,128)(2,1)} %broadcast_in_dim.53) | data formatting | bytes 8421376 | tf_op jit(solution)/shard_map/while/body/eval_jaxpr/cond/branch_1_fun/while/body/eval_jaxpr/reshape | solution.py:20
  219.6 2.2 slice-done
  221.8 1.1 copy.17
  223.0 0.5 bitcast_select_fusion.6
  223.6 2.0 fusion.21
  225.6 3.2 %broadcast_in_dim.53 = bf16[64,128,257]{2,1,0:T(8,128)(2,1)} broadcast(bf16[64,257]{1,0:T(8,128)(2,1)S(1)} %concatenate.14), dimensions={0,2} | broadcast | bytes 4243584 | tf_op jit(solution)/shard_map/while/body/eval_jaxpr/cond/branch_1_fun/while/body/eval_jaxpr/broadcast_in_dim | solution.py:19
  228.8 10.8 %reshape.107 = bf16[64,32896]{1,0:T(8,128)(2,1)} reshape(bf16[64,128,257]{2,1,0:T(8,128)(2,1)} %broadcast_in_dim.53) | data formatting | bytes 8421376 | tf_op jit(solution)/shard_map/while/body/eval_jaxpr/cond/branch_1_fun/while/body/eval_jaxpr/reshape | solution.py:20
  239.6 2.2 slice-done
  241.8 1.1 copy.17
  243.0 0.5 bitcast_select_fusion.6
  243.6 2.0 fusion.21
  245.6 3.2 %broadcast_in_dim.53 = bf16[64,128,257]{2,1,0:T(8,128)(2,1)} broadcast(bf16[64,257]{1,0:T(8,128)(2,1)S(1)} %concatenate.14), dimensions={0,2} | broadcast | bytes 4243584 | tf_op jit(solution)/shard_map/while/body/eval_jaxpr/cond/branch_1_fun/while/body/eval_jaxpr/broadcast_in_dim | solution.py:19
  248.8 10.8 %reshape.107 = bf16[64,32896]{1,0:T(8,128)(2,1)} reshape(bf16[64,128,257]{2,1,0:T(8,128)(2,1)} %broadcast_in_dim.53) | data formatting | bytes 8421376 | tf_op jit(solution)/shard_map/while/body/eval_jaxpr/cond/branch_1_fun/while/body/eval_jaxpr/reshape | solution.py:20
  259.6 2.2 slice-done
  261.8 1.1 copy.17
  263.0 0.5 bitcast_select_fusion.6
  263.6 2.0 fusion.21
  265.6 3.2 %broadcast_in_dim.53 = bf16[64,128,257]{2,1,0:T(8,128)(2,1)} broadcast(bf16[64,257]{1,0:T(8,128)(2,1)S(1)} %concatenate.14), dimensions={0,2} | broadcast | bytes 4243584 | tf_op jit(solution)/shard_map/while/body/eval_jaxpr/cond/branch_1_fun/while/body/eval_jaxpr/broadcast_in_dim | solution.py:19
  268.8 10.8 %reshape.107 = bf16[64,32896]{1,0:T(8,128)(2,1)} reshape(bf16[64,128,257]{2,1,0:T(8,128)(2,1)} %broadcast_in_dim.53) | data formatting | bytes 8421376 | tf_op jit(solution)/shard_map/while/body/eval_jaxpr/cond/branch_1_fun/while/body/eval_jaxpr/reshape | solution.py:20
  279.6 2.2 slice-done
  281.8 1.1 copy.17
  283.6 2.0 fusion.21
  285.6 2.1 fusion.6
  287.6 2.7 fusion.18
  290.4 2.3 copy.14
  (29 shorter events, 2.1 us)
Async XLA Ops:
  0.7 49.9 %collective-permute-start.2 = (s32[128]{0:T(128)S(1)}, s32[128]{0:T(128)S(1)}, u32[]{:S(2)}, u32[]{:S(2)}) collective-permute-start(s32[128]{0:T(128)S(1)} %fusion.11), channel_id=1, source_target_pairs={{1,0},{2,1},{3,2},{4,3},{5,4},{6,5},{7,6},{8,7},{9,8},{10,9},{11,1... | collective-permute-start | bytes 1544 | tf_op jit(solution)/shard_map/while/body/eval_jaxpr/ppermute | solution.py:10
  2.6 2.8 copy-start.1
  2.6 46.6 %copy-start = (bf16[1,1,128,4096]{3,2,1,0:T(8,128)(2,1)S(1)}, bf16[1,1,128,4096]{3,2,1,0:T(8,128)(2,1)}, u32[]{:S(2)}) copy-start(bf16[1,1,128,4096]{3,2,1,0:T(8,128)(2,1)} %param.10) | copy-start | bytes 3145732
  51.7 4.8 %collective-permute-start = (bf16[128,4096]{0,1:T(8,128)(2,1)}, bf16[128,4096]{0,1:T(8,128)(2,1)S(1)}, u32[]{:S(2)}, u32[]{:S(2)}) collective-permute-start(bf16[128,4096]{0,1:T(8,128)(2,1)} %get-tuple-element.528), channel_id=1, source_target_pairs={{16,0},{17,1},{18,2},{19,3},{20,4},{21,5},{22,6},{23,7},{24,8},{25... | collective-permute-start | bytes 3145736 | tf_op jit(solution)/shard_map/while/body/eval_jaxpr/ppermute | solution.py:10
  59.1 27.1 %collective-permute-start.1 = (bf16[128,4096]{0,1:T(8,128)(2,1)S(1)}, bf16[128,4096]{0,1:T(8,128)(2,1)S(1)}, u32[]{:S(2)}, u32[]{:S(2)}) collective-permute-start(bf16[128,4096]{0,1:T(8,128)(2,1)S(1)} %get-tuple-element.481), channel_id=1, source_target_pairs={{1,0},{2,1},{3,2},{4,3},{5,4},{6,5},{7,6},{8,7},{9,8},{10,9},{11,1... | collective-permute-start | bytes 3145736 | tf_op jit(solution)/shard_map/while/body/eval_jaxpr/ppermute | solution.py:10
  89.1 85.8 %collective-permute-start = (bf16[128,4096]{0,1:T(8,128)(2,1)}, bf16[128,4096]{0,1:T(8,128)(2,1)S(1)}, u32[]{:S(2)}, u32[]{:S(2)}) collective-permute-start(bf16[128,4096]{0,1:T(8,128)(2,1)} %get-tuple-element.528), channel_id=1, source_target_pairs={{16,0},{17,1},{18,2},{19,3},{20,4},{21,5},{22,6},{23,7},{24,8},{25... | collective-permute-start | bytes 3145736 | tf_op jit(solution)/shard_map/while/body/eval_jaxpr/ppermute | solution.py:10
  177.5 27.1 %collective-permute-start.1 = (bf16[128,4096]{0,1:T(8,128)(2,1)S(1)}, bf16[128,4096]{0,1:T(8,128)(2,1)S(1)}, u32[]{:S(2)}, u32[]{:S(2)}) collective-permute-start(bf16[128,4096]{0,1:T(8,128)(2,1)S(1)} %get-tuple-element.481), channel_id=1, source_target_pairs={{1,0},{2,1},{3,2},{4,3},{5,4},{6,5},{7,6},{8,7},{9,8},{10,9},{11,1... | collective-permute-start | bytes 3145736 | tf_op jit(solution)/shard_map/while/body/eval_jaxpr/ppermute | solution.py:10
  219.6 2.2 slice-start
  239.6 2.2 slice-start
  259.6 2.2 slice-start
  279.6 2.2 slice-start
where the time goes:
time: 294 us; the launch traced here: 293 us
  waiting for transfers between devices  140 us (48%)
  local copies, waits for them, and re-layouts  76.3 us (26%)
  blocking collectives  43.9 us (15%)
  other arithmetic  18.2 us (6%)
  matrix products  8.04 us (3%)
  starting transfers between devices  6.4 us (2%)
    ppermute x5, waiting for transfers between devices, passed_along(): return lax.ppermute(value, axis, pairs)  140 us
    all_gather x1, blocking collectives, body(): filt_all = lax.all_gather(filters, 'dp', axis=1, tiled=True)[0]  43.9 us
    reshape x4, local copies, waits for them, and re-layouts, band_table(): tiled_rows = tiled_rows.reshape(groups, tap_count * (span_cols + 1))  43.4 us
    broadcast_in_dim x4, local copies, waits for them, and re-layouts, band_table(): jnp.broadcast_to(base_row[:, None, :], (groups, tap_count, span_cols + 1))  12.8 us
    slice x8, local copies, waits for them, and re-layouts, band_table(): tiled_rows[:, :tap_count * span_cols].reshape(groups, tap_count, span_cols)  8.75 us
    dot_general x4, matrix products, one_block(): jnp.einsum('rgtj,rjgc->rtgc', masked, slab_piece, preferred_element_type=...  8.04 us
    ppermute x5, starting transfers between devices, passed_along(): return lax.ppermute(value, axis, pairs)  6.4 us
  transfers between devices with their start and end apart: 5, of which 4 were waited for; matrix products, arithmetic and copies ran while one was open for 2% of the time, Pallas kernels for 0%

commit v1 on v0

v1 whole, which is shorter than its diff:
```python
import functools

import jax
import jax.numpy as jnp
from jax import lax
from jax.experimental import pallas as pl
from jax.experimental.pallas import tpu as pltpu
from jax.sharding import PartitionSpec as P

MESH_ID = pl.DeviceIdType.MESH
CHUNK = 256
LAG = 2


def kernel(
    dp_count, pipe_count, lane_width, slot_groups,
    gate, filt, docs, loss, out,
    gbuf, inc, sbuf, halo, obuf, fall, table, docs_own, docs_next, mask_own, mask_next,
    gsem, lsem, osem, fsend, frecv, hsend, hrecv, psend, precv, dsend, drecv,
):
    chunk_count, rows, width = sbuf.shape
    groups = width // lane_width
    slots = groups // slot_groups
    stage = lax.axis_index("pipe")
    me = lax.axis_index("dp")
    is_last_stage = stage == pipe_count - 1
    not_last_stage = stage < pipe_count - 1
    has_below = stage > 0
    has_before = me > 0
    has_next = me < dp_count - 1

    def columns(j):
        return pl.ds(pl.multiple_of(j * width, width), width)

    def gate_copy(j):
        return pltpu.make_async_copy(gate.at[0, 0, :, columns(j)], gbuf.at[j], gsem.at[j])

    def loss_copy(j):
        return pltpu.make_async_copy(loss.at[0, :, columns(j)], inc.at[j], lsem.at[j])

    def out_copy(j):
        return pltpu.make_async_copy(obuf.at[j], out.at[0, 0, :, columns(j)], osem.at[j])

    def filter_copy(slot, peer):
        return pltpu.make_async_remote_copy(
            src_ref=filt, dst_ref=fall.at[slot], send_sem=fsend.at[peer], recv_sem=frecv.at[slot],
            device_id=(stage, peer), device_id_type=MESH_ID,
        )

    def halo_copy(j):
        return pltpu.make_async_remote_copy(
            src_ref=sbuf.at[j], dst_ref=halo.at[j], send_sem=hsend.at[j], recv_sem=hrecv.at[j],
            device_id=(stage, me - 1), device_id_type=MESH_ID,
        )

    def docs_copy():
        return pltpu.make_async_remote_copy(
            src_ref=docs_own, dst_ref=docs_next, send_sem=dsend, recv_sem=drecv,
            device_id=(stage, me - 1), device_id_type=MESH_ID,
        )

    def pipe_copy(j):
        return pltpu.make_async_remote_copy(
            src_ref=obuf.at[j], dst_ref=inc.at[j], send_sem=psend.at[j], recv_sem=precv.at[j],
            device_id=(stage - 1, me), device_id_type=MESH_ID,
        )

    def each(count, fn):
        def step(j, carry):
            fn(j)
            return carry
        lax.fori_loop(0, count, step, 0)

    each(chunk_count, lambda j: gate_copy(j).start())

    @pl.when(is_last_stage)
    def _():
        each(chunk_count, lambda j: loss_copy(j).start())

    barrier = pltpu.get_barrier_semaphore()

    def greet(k):
        pl.semaphore_signal(
            barrier, inc=1, device_id=(stage, lax.rem(me + k + 1, dp_count)), device_id_type=MESH_ID
        )

    each(dp_count - 1, greet)

    @pl.when(has_below)
    def _():
        pl.semaphore_signal(barrier, inc=1, device_id=(stage - 1, me), device_id_type=MESH_ID)

    @pl.when(not_last_stage)
    def _():
        pl.semaphore_signal(barrier, inc=1, device_id=(stage + 1, me), device_id_type=MESH_ID)

    docs_own[...] = jnp.broadcast_to(docs[...], docs_own.shape)
    fall[me] = filt[...]

    greeted = dp_count - 1 + has_below.astype(jnp.int32) + not_last_stage.astype(jnp.int32)
    pl.semaphore_wait(barrier, greeted)

    def send_filters(k):
        peer = lax.rem(me + k + 1, dp_count)
        filter_copy(me, peer).start()

    @pl.when(has_before)
    def _():
        docs_copy().start()

    each(dp_count - 1, send_filters)

    def scale(j):
        gate_copy(j).wait()

        @pl.when(is_last_stage)
        def _():
            loss_copy(j).wait()

        @pl.when(not_last_stage)
        def _():
            pltpu.make_async_remote_copy(
                src_ref=obuf.at[j], dst_ref=inc.at[j], send_sem=psend.at[j], recv_sem=precv.at[j],
                device_id=(stage + 1, me), device_id_type=MESH_ID,
            ).wait_recv()

        sbuf[j] = (gbuf[j].astype(jnp.float32) * inc[j].astype(jnp.float32)).astype(jnp.bfloat16)

        @pl.when(has_before)
        def _():
            halo_copy(j).start()

    @pl.when(is_last_stage)
    def _():
        each(chunk_count, scale)

    @pl.when(jnp.logical_not(has_next))
    def _():
        docs_next[...] = jnp.zeros_like(docs_next)

        def clear(j):
            halo[j] = jnp.zeros((rows, width), jnp.bfloat16)

        each(chunk_count, clear)

    @pl.when(has_next)
    def _():
        pltpu.make_async_remote_copy(
            src_ref=docs_own, dst_ref=docs_next, send_sem=dsend, recv_sem=drecv,
            device_id=(stage, me + 1), device_id_type=MESH_ID,
        ).wait_recv()

    at_row = lax.broadcasted_iota(jnp.int32, (rows, rows), 0)
    at_col = lax.broadcasted_iota(jnp.int32, (rows, rows), 1)
    own_cols = jnp.broadcast_to(docs_own[0:1, :], (rows, rows)).astype(jnp.float32)
    next_cols = jnp.broadcast_to(docs_next[0:1, :], (rows, rows)).astype(jnp.float32)
    own_rows = own_cols.T
    one, zero = jnp.float32(1.0), jnp.float32(0.0)
    mask_own[...] = jnp.where(
        jnp.logical_and(at_col >= at_row, own_rows == own_cols), one, zero
    ).astype(jnp.bfloat16)
    mask_next[...] = jnp.where(
        jnp.logical_and(at_col < at_row, own_rows == next_cols), one, zero
    ).astype(jnp.bfloat16)

    def make_table(j):
        for q in range(slots):
            slot = j * slots + q

            @pl.when(slot != me)
            def _():
                filter_copy(slot, slot).wait_recv()

        for q in range(slots):
            taps = fall[j * slots + q].astype(jnp.float32)
            for r in range(slot_groups):
                g = q * slot_groups + r
                spread = jnp.broadcast_to(taps[r : r + 1, :], (rows, rows))
                turned = pltpu.roll(spread, 0, 1, stride=1, stride_axis=0).astype(jnp.bfloat16)
                table[g * rows : (g + 1) * rows, :rows] = turned * mask_own[...]
                table[g * rows : (g + 1) * rows, rows:] = turned * mask_next[...]

    def produce(j):
        @pl.when(has_next)
        def _():
            pltpu.make_async_remote_copy(
                src_ref=sbuf.at[j], dst_ref=halo.at[j], send_sem=hsend.at[j], recv_sem=hrecv.at[j],
                device_id=(stage, me + 1), device_id_type=MESH_ID,
            ).wait_recv()

        slab = jnp.concatenate([sbuf[j], halo[j]], axis=0)
        group_of = lax.broadcasted_iota(jnp.int32, (rows, width), 1) // lane_width
        total = inc[j].astype(jnp.float32)
        update = jnp.zeros((rows, width), jnp.float32)
        for g in range(groups):
            part = jnp.dot(
                table[g * rows : (g + 1) * rows, :], slab, preferred_element_type=jnp.float32
            )
            update = jnp.where(group_of == g, part, update)
        obuf[j] = (total + update).astype(jnp.bfloat16)

        @pl.when(has_below)
        def _():
            pipe_copy(j).start()

        out_copy(j).start()

    def step(s):
        @pl.when(s >= LAG)
        def _():
            make_table(s - LAG)

        @pl.when(jnp.logical_and(not_last_stage, s < chunk_count))
        def _():
            scale(s)

        @pl.when(s >= LAG)
        def _():
            produce(s - LAG)

    each(chunk_count + LAG, step)

    def finish(j):
        out_copy(j).wait()

        @pl.when(has_below)
        def _():
            pipe_copy(j).wait_send()

        @pl.when(has_before)
        def _():
            halo_copy(j).wait_send()

    each(chunk_count, finish)

    @pl.when(has_before)
    def _():
        docs_copy().wait_send()

    each(dp_count - 1, lambda k: filter_copy(me, lax.rem(me + k + 1, dp_count)).wait_send())


def body(mesh_shape, gate, filters, doc_ids, loss_grad):
    dp_count, pipe_count = mesh_shape["dp"], mesh_shape["pipe"]
    _, _, rows, channels = gate.shape
    slot_groups, taps = filters.shape[1:]
    lane_width = channels // (slot_groups * dp_count)
    chunk_count = channels // CHUNK
    slot_rows = -(-slot_groups // 16) * 16
    filt = filters[0]
    if slot_rows != slot_groups:
        filt = jnp.pad(filt, ((0, slot_rows - slot_groups), (0, 0)))
    chunks = pltpu.VMEM((chunk_count, rows, CHUNK), jnp.bfloat16)
    groups = CHUNK // lane_width
    dma = pltpu.SemaphoreType.DMA
    return pl.pallas_call(
        functools.partial(kernel, dp_count, pipe_count, lane_width, slot_groups),
        out_shape=jax.ShapeDtypeStruct(gate.shape, jnp.bfloat16),
        in_specs=[
            pl.BlockSpec(memory_space=pl.ANY),
            pl.BlockSpec(memory_space=pltpu.VMEM),
            pl.BlockSpec(memory_space=pltpu.VMEM),
            pl.BlockSpec(memory_space=pl.ANY),
        ],
        out_specs=pl.BlockSpec(memory_space=pl.ANY),
        scratch_shapes=[
            chunks, chunks, chunks, chunks, chunks,
            pltpu.VMEM((dp_count, slot_rows, taps), jnp.bfloat16),
            pltpu.VMEM((groups * rows, 2 * rows), jnp.bfloat16),
            pltpu.VMEM((8, rows), jnp.int32),
            pltpu.VMEM((8, rows), jnp.int32),
            pltpu.VMEM((rows, rows), jnp.bfloat16),
            pltpu.VMEM((rows, rows), jnp.bfloat16),
            dma((chunk_count,)), dma((chunk_count,)), dma((chunk_count,)),
            dma((dp_count,)), dma((dp_count,)),
            dma((chunk_count,)), dma((chunk_count,)),
            dma((chunk_count,)), dma((chunk_count,)),
            dma, dma,
        ],
        compiler_params=pltpu.CompilerParams(
            collective_id=0, has_side_effects=True, vmem_limit_bytes=40 * 1024 * 1024
        ),
        cost_estimate=pl.CostEstimate(
            flops=2 * 2 * rows * rows * channels * 16, bytes_accessed=6 * rows * channels, transcendentals=0
        ),
    )(gate, filt, doc_ids, loss_grad)


def solution(mesh):
    return jax.shard_map(
        functools.partial(body, dict(mesh.shape)),
        mesh=mesh,
        in_specs=(
            P("pipe", None, "dp", None),
            P("pipe", "dp", None),
            P(None, "dp"),
            P(None, "dp", None),
        ),
        out_specs=P("pipe", None, "dp", None),
        check_vma=False,
    )
```

time: 294 us -> 45.3 us (0.15)
  waiting for transfers between devices: 140 us -> 0 us
  local copies, waits for them, and re-layouts: 76.3 us -> 4.76 us
  blocking collectives: 43.9 us -> 0 us
  Pallas kernels: 0 us -> 40.3 us
  other arithmetic: 18.2 us -> 0 us
  matrix products: 8.04 us -> 0 us
  starting transfers between devices: 6.4 us -> 0 us
    ppermute x5 -> x0, waiting for transfers between devices: 140 us -> none  [passed_along(): return lax.ppermute(value, axis, pairs)]
    all_gather x1 -> x0, blocking collectives: 43.9 us -> none  [body(): filt_all = lax.all_gather(filters, 'dp', axis=1, tiled=True)[0]]
    reshape x5 -> x0, local copies, waits for them, and re-layouts: 43.8 us -> none  [the longest x4 43.4 us: band_table(): tiled_rows = tiled_rows.reshape(groups, tap_count * (span_cols + 1))]
    pallas_call x0 -> x1, Pallas kernels: none -> 40.3 us  [body(): pl.pallas_call(functools.partial(kernel, dp_count, pipe_count, lane_width...]
    broadcast_in_dim x4 -> x0, local copies, waits for them, and re-layouts: 12.8 us -> none  [band_table(): jnp.broadcast_to(base_row[:, None, :], (groups, tap_count, span_cols + 1))]
    slice x8 -> x0, local copies, waits for them, and re-layouts: 8.75 us -> none  [band_table(): tiled_rows[:, :tap_count * span_cols].reshape(groups, tap_count, span_cols)]
    dot_general x4 -> x0, matrix products: 8.04 us -> none  [one_block(): jnp.einsum('rgtj,rjgc->rtgc', masked, slab_piece, preferred_element_type=...]
    convert_element_type x3 -> x0, other arithmetic: 7.4 us -> none  [the longest x2 5.34 us: one_tick(): (gate_now.astype(jnp.float32) * incoming.astype(jnp.float32)).astype(jnp....]
  transfers between devices with their start and end apart: 5 -> 0, of which waited for: 4 -> 0; matrix products, arithmetic and copies ran while one was open for 2% -> 0% of each run, Pallas kernels for 0% -> 0%
where the time goes in v1:
time: 45.3 us; the launch traced here: 45.1 us
  Pallas kernels  40.3 us (89%)
  local copies, waits for them, and re-layouts  4.76 us (11%)
    pallas_call x1, Pallas kernels, body(): pl.pallas_call(functools.partial(kernel, dp_count, pipe_count, lane_width...  40.3 us
    unnamed x9, local copies, waits for them, and re-layouts  4.76 us

profile of v1, /device:TPU:0, one launch (start us, length us, event | category | flops | bytes accessed | tf_op | source)
XLA Modules:
  0.0 45.1 jit_solution(13019648167856092822)
XLA Ops:
  0.0 0.0 copy-start.3
  0.0 0.7 %copy-done.3 = s32[1,128]{1,0:T(1,128)S(1)} copy-done((s32[1,128]{1,0:T(1,128)S(1)}, s32[1,128]{1,0:T(1,128)}, u32[]{:S(2)}) %copy-start.3) | copy-done | bytes 536
  0.7 0.0 copy-start
  0.7 1.2 %copy-done = bf16[1,1,128,4096]{3,2,1,0:T(8,128)(2,1)S(1)} copy-done((bf16[1,1,128,4096]{3,2,1,0:T(8,128)(2,1)S(1)}, bf16[1,1,128,4096]{3,2,1,0:T(8,128)(2,1)}, u32[]{:S(2)}) %copy-start) | copy-done | bytes 1048600
  1.9 0.0 copy-start.1
  1.9 1.2 %copy-done.1 = bf16[1,128,4096]{2,1,0:T(8,128)(2,1)S(1)} copy-done((bf16[1,128,4096]{2,1,0:T(8,128)(2,1)S(1)}, bf16[1,128,4096]{2,1,0:T(8,128)(2,1)}, u32[]{:S(2)}) %copy-start.1) | copy-done | bytes 1048600
  3.1 0.0 copy-start.2
  3.1 0.7 %copy-done.2 = bf16[1,16,128]{2,1,0:T(8,128)(2,1)S(1)} copy-done((bf16[1,16,128]{2,1,0:T(8,128)(2,1)S(1)}, bf16[1,16,128]{2,1,0:T(8,128)(2,1)}, u32[]{:S(2)}) %copy-start.2) | copy-done | bytes 4120
  3.8 40.3 %shard_map.46 = bf16[1,1,128,4096]{3,2,1,0:T(8,128)(2,1)S(1)} custom-call(bf16[1,1,128,4096]{3,2,1,0:T(8,128)(2,1)S(1)} %copy-done, bf16[16,128]{1,0:T(8,128)(2,1)S(1)} %bitcast.1, s32[1,128]{1,0:T(1,128)S(1)} %copy-done.3, bf16[1,128,4096]{2,1,0:T(8,128)(2,1)S(1)} %copy-done.1), custom_call_target="tpu_custom_call" | custom-call | flops 4294967296 | bytes 3145728 | tf_op jit(solution)/shard_map/pallas_call | solution.py:256
  44.1 1.0 %copy.6 = bf16[1,1,128,4096]{3,2,1,0:T(8,128)(2,1)} copy(bf16[1,1,128,4096]{3,2,1,0:T(8,128)(2,1)S(1)} %shard_map.46) | data formatting | bytes 2097152
Async XLA Ops:
  0.0 0.7 %copy-start.3 = (s32[1,128]{1,0:T(1,128)S(1)}, s32[1,128]{1,0:T(1,128)}, u32[]{:S(2)}) copy-start(s32[1,128]{1,0:T(1,128)} %docs.1) | copy-start | bytes 1540
  0.7 1.2 %copy-start = (bf16[1,1,128,4096]{3,2,1,0:T(8,128)(2,1)S(1)}, bf16[1,1,128,4096]{3,2,1,0:T(8,128)(2,1)}, u32[]{:S(2)}) copy-start(bf16[1,1,128,4096]{3,2,1,0:T(8,128)(2,1)} %gate.1) | copy-start | bytes 3145732
  1.9 1.2 %copy-start.1 = (bf16[1,128,4096]{2,1,0:T(8,128)(2,1)S(1)}, bf16[1,128,4096]{2,1,0:T(8,128)(2,1)}, u32[]{:S(2)}) copy-start(bf16[1,128,4096]{2,1,0:T(8,128)(2,1)} %loss.1) | copy-start | bytes 3145732
  3.1 0.7 %copy-start.2 = (bf16[1,16,128]{2,1,0:T(8,128)(2,1)S(1)}, bf16[1,16,128]{2,1,0:T(8,128)(2,1)}, u32[]{:S(2)}) copy-start(bf16[1,16,128]{2,1,0:T(8,128)(2,1)} %param.5) | copy-start | bytes 12292

commit v2 on v1

--- a/solution.py
+++ b/solution.py
@@ -9,13 +9,13 @@
 
 MESH_ID = pl.DeviceIdType.MESH
 CHUNK = 256
-LAG = 2
+LAG = 5
 
 
 def kernel(
     dp_count, pipe_count, lane_width, slot_groups,
-    gate, filt, docs, loss, out,
-    gbuf, inc, sbuf, halo, obuf, fall, table, docs_own, docs_next, mask_own, mask_next,
+    gate, filt_hbm, docs_hbm, loss, out,
+    filt, docs, filt_sem, docs_sem, gbuf, inc, sbuf, halo, obuf, fall, table, docs_own, docs_next, mask_own, mask_next,
     gsem, lsem, osem, fsend, frecv, hsend, hrecv, psend, precv, dsend, drecv,
 ):
     chunk_count, rows, width = sbuf.shape
@@ -71,6 +71,10 @@
             return carry
         lax.fori_loop(0, count, step, 0)
 
+    load_filters = pltpu.make_async_copy(filt_hbm, filt, filt_sem)
+    load_docs = pltpu.make_async_copy(docs_hbm, docs, docs_sem)
+    load_filters.start()
+    load_docs.start()
     each(chunk_count, lambda j: gate_copy(j).start())
 
     @pl.when(is_last_stage)
@@ -94,6 +98,8 @@
     def _():
         pl.semaphore_signal(barrier, inc=1, device_id=(stage + 1, me), device_id_type=MESH_ID)
 
+    load_filters.wait()
+    load_docs.wait()
     docs_own[...] = jnp.broadcast_to(docs[...], docs_own.shape)
     fall[me] = filt[...]
 
@@ -192,11 +198,9 @@
         group_of = lax.broadcasted_iota(jnp.int32, (rows, width), 1) // lane_width
         total = inc[j].astype(jnp.float32)
         update = jnp.zeros((rows, width), jnp.float32)
+        parts = jnp.dot(table[...], slab, preferred_element_type=jnp.float32)
         for g in range(groups):
-            part = jnp.dot(
-                table[g * rows : (g + 1) * rows, :], slab, preferred_element_type=jnp.float32
-            )
-            update = jnp.where(group_of == g, part, update)
+            update = jnp.where(group_of == g, parts[g * rows : (g + 1) * rows, :], update)
         obuf[j] = (total + update).astype(jnp.bfloat16)
 
         @pl.when(has_below)
@@ -258,12 +262,15 @@
         out_shape=jax.ShapeDtypeStruct(gate.shape, jnp.bfloat16),
         in_specs=[
             pl.BlockSpec(memory_space=pl.ANY),
-            pl.BlockSpec(memory_space=pltpu.VMEM),
-            pl.BlockSpec(memory_space=pltpu.VMEM),
+            pl.BlockSpec(memory_space=pl.ANY),
+            pl.BlockSpec(memory_space=pl.ANY),
             pl.BlockSpec(memory_space=pl.ANY),
         ],
         out_specs=pl.BlockSpec(memory_space=pl.ANY),
         scratch_shapes=[
+            pltpu.VMEM((slot_rows, taps), jnp.bfloat16),
+            pltpu.VMEM((1, rows), jnp.int32),
+            dma, dma,
             chunks, chunks, chunks, chunks, chunks,
             pltpu.VMEM((dp_count, slot_rows, taps), jnp.bfloat16),
             pltpu.VMEM((groups * rows, 2 * rows), jnp.bfloat16),
@@ -278,7 +285,7 @@
             dma, dma,
         ],
         compiler_params=pltpu.CompilerParams(
-            collective_id=0, has_side_effects=True, vmem_limit_bytes=40 * 1024 * 1024
+            collective_id=0, has_side_effects=True, vmem_limit_bytes=62 * 1024 * 1024
         ),
         cost_estimate=pl.CostEstimate(
             flops=2 * 2 * rows * rows * channels * 16, bytes_accessed=6 * rows * channels, transcendentals=0

time: 45.3 us -> 37.2 us (0.82)
  Pallas kernels: 40.3 us -> 34.7 us
  local copies, waits for them, and re-layouts: 4.76 us -> 2.29 us
    pallas_call x1, Pallas kernels: 40.3 us -> 34.7 us  [body(): pl.pallas_call(functools.partial(kernel, dp_count, pipe_count, lane_width...]
    unnamed x9 -> x1, local copies, waits for them, and re-layouts: 4.76 us -> 2.29 us
where the time goes in v2:
time: 37.2 us; the launch traced here: 37 us
  Pallas kernels  34.7 us (93%)
  local copies, waits for them, and re-layouts  2.29 us (6%)
    pallas_call x1, Pallas kernels, body(): pl.pallas_call(functools.partial(kernel, dp_count, pipe_count, lane_width...  34.7 us
    unnamed x1, local copies, waits for them, and re-layouts  2.29 us

profile of v2, /device:TPU:0, one launch (start us, length us, event | category | flops | bytes accessed | tf_op | source)
XLA Modules:
  0.0 37.0 jit_solution(6050566257786046920)
XLA Ops:
  0.0 34.7 %shard_map.46 = bf16[1,1,128,4096]{3,2,1,0:T(8,128)(2,1)} custom-call(bf16[1,1,128,4096]{3,2,1,0:T(8,128)(2,1)} %gate.1, bf16[16,128]{1,0:T(8,128)(2,1)} %bitcast.1, s32[1,128]{1,0:T(1,128)} %docs_hbm.1, bf16[1,128,4096]{2,1,0:T(8,128)(2,1)} %loss.1), custom_call_target="tpu_custom_call" | custom-call | flops 4294967296 | bytes 3145728 | tf_op jit(solution)/shard_map/pallas_call | solution.py:260
  34.8 2.3 %copy.6 = bf16[1,1,128,4096]{3,2,1,0:T(8,128)(2,1)} copy(bf16[1,1,128,4096]{3,2,1,0:T(8,128)(2,1)} %shard_map.46) | data formatting | bytes 2097152

commit v3 on v2

--- a/solution.py
+++ b/solution.py
@@ -181,10 +181,12 @@
             taps = fall[j * slots + q].astype(jnp.float32)
             for r in range(slot_groups):
                 g = q * slot_groups + r
-                spread = jnp.broadcast_to(taps[r : r + 1, :], (rows, rows))
-                turned = pltpu.roll(spread, 0, 1, stride=1, stride_axis=0).astype(jnp.bfloat16)
-                table[g * rows : (g + 1) * rows, :rows] = turned * mask_own[...]
-                table[g * rows : (g + 1) * rows, rows:] = turned * mask_next[...]
+                spread = jnp.broadcast_to(taps[r : r + 1, :], (8, rows))
+                first = pltpu.roll(spread, 0, 1, stride=1, stride_axis=0)
+                pieces = [first] + [pltpu.roll(first, row, 1) for row in range(8, rows, 8)]
+                turned = jnp.concatenate(pieces, axis=0).astype(jnp.bfloat16)
+                table[j, g * rows : (g + 1) * rows, :rows] = turned * mask_own[...]
+                table[j, g * rows : (g + 1) * rows, rows:] = turned * mask_next[...]
 
     def produce(j):
         @pl.when(has_next)
@@ -198,7 +200,7 @@
         group_of = lax.broadcasted_iota(jnp.int32, (rows, width), 1) // lane_width
         total = inc[j].astype(jnp.float32)
         update = jnp.zeros((rows, width), jnp.float32)
-        parts = jnp.dot(table[...], slab, preferred_element_type=jnp.float32)
+        parts = jnp.dot(table[j], slab, preferred_element_type=jnp.float32)
         for g in range(groups):
             update = jnp.where(group_of == g, parts[g * rows : (g + 1) * rows, :], update)
         obuf[j] = (total + update).astype(jnp.bfloat16)
@@ -209,20 +211,22 @@
 
         out_copy(j).start()
 
+    lag = LAG - (LAG - 1) * is_last_stage.astype(jnp.int32)
+
     def step(s):
-        @pl.when(s >= LAG)
-        def _():
-            make_table(s - LAG)
+        @pl.when(s < chunk_count)
+        def _():
+            make_table(s)
 
         @pl.when(jnp.logical_and(not_last_stage, s < chunk_count))
         def _():
             scale(s)
 
-        @pl.when(s >= LAG)
-        def _():
-            produce(s - LAG)
-
-    each(chunk_count + LAG, step)
+        @pl.when(s >= lag)
+        def _():
+            produce(s - lag)
+
+    each(chunk_count + lag, step)
 
     def finish(j):
         out_copy(j).wait()
@@ -273,7 +277,7 @@
             dma, dma,
             chunks, chunks, chunks, chunks, chunks,
             pltpu.VMEM((dp_count, slot_rows, taps), jnp.bfloat16),
-            pltpu.VMEM((groups * rows, 2 * rows), jnp.bfloat16),
+            pltpu.VMEM((chunk_count, groups * rows, 2 * rows), jnp.bfloat16),
             pltpu.VMEM((8, rows), jnp.int32),
             pltpu.VMEM((8, rows), jnp.int32),
             pltpu.VMEM((rows, rows), jnp.bfloat16),

time: 37.2 us -> 36.9 us (level)
  no operation moved by 1% of the time
where the time goes in v3:
time: 36.9 us; the launch traced here: 36.7 us
  Pallas kernels  34.4 us (93%)
  local copies, waits for them, and re-layouts  2.29 us (6%)
    pallas_call x1, Pallas kernels, body(): pl.pallas_call(functools.partial(kernel, dp_count, pipe_count, lane_width...  34.4 us
    unnamed x1, local copies, waits for them, and re-layouts  2.29 us

profile of v3, /device:TPU:0, one launch (start us, length us, event | category | flops | bytes accessed | tf_op | source)
XLA Modules:
  0.0 36.7 jit_solution(738529537460048220)
XLA Ops:
  0.0 34.4 %shard_map.46 = bf16[1,1,128,4096]{3,2,1,0:T(8,128)(2,1)} custom-call(bf16[1,1,128,4096]{3,2,1,0:T(8,128)(2,1)} %gate.1, bf16[16,128]{1,0:T(8,128)(2,1)} %bitcast.1, s32[1,128]{1,0:T(1,128)} %docs_hbm.1, bf16[1,128,4096]{2,1,0:T(8,128)(2,1)} %loss.1), custom_call_target="tpu_custom_call" | custom-call | flops 4294967296 | bytes 3145728 | tf_op jit(solution)/shard_map/pallas_call | solution.py:264
  34.4 2.3 %copy.6 = bf16[1,1,128,4096]{3,2,1,0:T(8,128)(2,1)} copy(bf16[1,1,128,4096]{3,2,1,0:T(8,128)(2,1)} %shard_map.46) | data formatting | bytes 2097152

commit v4 on v3

--- a/solution.py
+++ b/solution.py
@@ -9,7 +9,7 @@
 
 MESH_ID = pl.DeviceIdType.MESH
 CHUNK = 256
-LAG = 5
+LAG = 4
 
 
 def kernel(
@@ -181,10 +181,8 @@
             taps = fall[j * slots + q].astype(jnp.float32)
             for r in range(slot_groups):
                 g = q * slot_groups + r
-                spread = jnp.broadcast_to(taps[r : r + 1, :], (8, rows))
-                first = pltpu.roll(spread, 0, 1, stride=1, stride_axis=0)
-                pieces = [first] + [pltpu.roll(first, row, 1) for row in range(8, rows, 8)]
-                turned = jnp.concatenate(pieces, axis=0).astype(jnp.bfloat16)
+                spread = jnp.broadcast_to(taps[r : r + 1, :], (rows, rows))
+                turned = pltpu.roll(spread, 0, 1, stride=1, stride_axis=0).astype(jnp.bfloat16)
                 table[j, g * rows : (g + 1) * rows, :rows] = turned * mask_own[...]
                 table[j, g * rows : (g + 1) * rows, rows:] = turned * mask_next[...]
 
@@ -211,7 +209,7 @@
 
         out_copy(j).start()
 
-    lag = LAG - (LAG - 1) * is_last_stage.astype(jnp.int32)
+    lag = LAG * not_last_stage.astype(jnp.int32)
 
     def step(s):
         @pl.when(s < chunk_count)

time: 36.9 us -> 37.3 us (1.011)
  Pallas kernels: 34.4 us -> 34.8 us
where the time goes in v4:
time: 37.3 us; the launch traced here: 37.1 us
  Pallas kernels  34.8 us (93%)
  local copies, waits for them, and re-layouts  2.29 us (6%)
    pallas_call x1, Pallas kernels, body(): pl.pallas_call(functools.partial(kernel, dp_count, pipe_count, lane_width...  34.8 us
    unnamed x1, local copies, waits for them, and re-layouts  2.29 us

profile of v4, /device:TPU:0, one launch (start us, length us, event | category | flops | bytes accessed | tf_op | source)
XLA Modules:
  0.0 37.1 jit_solution(14799489152634021796)
XLA Ops:
  0.0 34.8 %shard_map.46 = bf16[1,1,128,4096]{3,2,1,0:T(8,128)(2,1)} custom-call(bf16[1,1,128,4096]{3,2,1,0:T(8,128)(2,1)} %gate.1, bf16[16,128]{1,0:T(8,128)(2,1)} %bitcast.1, s32[1,128]{1,0:T(1,128)} %docs_hbm.1, bf16[1,128,4096]{2,1,0:T(8,128)(2,1)} %loss.1), custom_call_target="tpu_custom_call" | custom-call | flops 4294967296 | bytes 3145728 | tf_op jit(solution)/shard_map/pallas_call | solution.py:262
  34.8 2.3 %copy.6 = bf16[1,1,128,4096]{3,2,1,0:T(8,128)(2,1)} copy(bf16[1,1,128,4096]{3,2,1,0:T(8,128)(2,1)} %shard_map.46) | data formatting | bytes 2097152

commit v5 on v4

--- a/solution.py
+++ b/solution.py
@@ -10,12 +10,13 @@
 MESH_ID = pl.DeviceIdType.MESH
 CHUNK = 256
 LAG = 4
+DOT_GROUPS = 4
 
 
 def kernel(
     dp_count, pipe_count, lane_width, slot_groups,
     gate, filt_hbm, docs_hbm, loss, out,
-    filt, docs, filt_sem, docs_sem, gbuf, inc, sbuf, halo, obuf, fall, table, docs_own, docs_next, mask_own, mask_next,
+    filt, docs, filt_sem, docs_sem, gbuf, inc, sbuf, halo, obuf, fall, docs_own, docs_next, mask_own, mask_next,
     gsem, lsem, osem, fsend, frecv, hsend, hrecv, psend, precv, dsend, drecv,
 ):
     chunk_count, rows, width = sbuf.shape
@@ -169,7 +170,7 @@
         jnp.logical_and(at_col < at_row, own_rows == next_cols), one, zero
     ).astype(jnp.bfloat16)
 
-    def make_table(j):
+    def wait_filters(j):
         for q in range(slots):
             slot = j * slots + q
 
@@ -177,16 +178,10 @@
             def _():
                 filter_copy(slot, slot).wait_recv()
 
-        for q in range(slots):
-            taps = fall[j * slots + q].astype(jnp.float32)
-            for r in range(slot_groups):
-                g = q * slot_groups + r
-                spread = jnp.broadcast_to(taps[r : r + 1, :], (rows, rows))
-                turned = pltpu.roll(spread, 0, 1, stride=1, stride_axis=0).astype(jnp.bfloat16)
-                table[j, g * rows : (g + 1) * rows, :rows] = turned * mask_own[...]
-                table[j, g * rows : (g + 1) * rows, rows:] = turned * mask_next[...]
 
     def produce(j):
+        wait_filters(j)
+
         @pl.when(has_next)
         def _():
             pltpu.make_async_remote_copy(
@@ -198,9 +193,23 @@
         group_of = lax.broadcasted_iota(jnp.int32, (rows, width), 1) // lane_width
         total = inc[j].astype(jnp.float32)
         update = jnp.zeros((rows, width), jnp.float32)
-        parts = jnp.dot(table[j], slab, preferred_element_type=jnp.float32)
-        for g in range(groups):
-            update = jnp.where(group_of == g, parts[g * rows : (g + 1) * rows, :], update)
+        taps = [fall[j * slots + q].astype(jnp.float32) for q in range(slots)]
+        for start in range(0, groups, DOT_GROUPS):
+            tables = []
+            for g in range(start, start + DOT_GROUPS):
+                q, r = divmod(g, slot_groups)
+                spread = jnp.broadcast_to(taps[q][r : r + 1, :], (rows, rows))
+                turned = pltpu.roll(spread, 0, 1, stride=1, stride_axis=0).astype(jnp.bfloat16)
+                tables.append(
+                    jnp.concatenate([turned * mask_own[...], turned * mask_next[...]], axis=1)
+                )
+            parts = jnp.dot(
+                jnp.concatenate(tables, axis=0), slab, preferred_element_type=jnp.float32
+            )
+            for k in range(DOT_GROUPS):
+                update = jnp.where(
+                    group_of == start + k, parts[k * rows : (k + 1) * rows, :], update
+                )
         obuf[j] = (total + update).astype(jnp.bfloat16)
 
         @pl.when(has_below)
@@ -212,10 +221,6 @@
     lag = LAG * not_last_stage.astype(jnp.int32)
 
     def step(s):
-        @pl.when(s < chunk_count)
-        def _():
-            make_table(s)
-
         @pl.when(jnp.logical_and(not_last_stage, s < chunk_count))
         def _():
             scale(s)
@@ -257,7 +262,6 @@
     if slot_rows != slot_groups:
         filt = jnp.pad(filt, ((0, slot_rows - slot_groups), (0, 0)))
     chunks = pltpu.VMEM((chunk_count, rows, CHUNK), jnp.bfloat16)
-    groups = CHUNK // lane_width
     dma = pltpu.SemaphoreType.DMA
     return pl.pallas_call(
         functools.partial(kernel, dp_count, pipe_count, lane_width, slot_groups),
@@ -275,7 +279,6 @@
             dma, dma,
             chunks, chunks, chunks, chunks, chunks,
             pltpu.VMEM((dp_count, slot_rows, taps), jnp.bfloat16),
-            pltpu.VMEM((chunk_count, groups * rows, 2 * rows), jnp.bfloat16),
             pltpu.VMEM((8, rows), jnp.int32),
             pltpu.VMEM((8, rows), jnp.int32),
             pltpu.VMEM((rows, rows), jnp.bfloat16),

time: 37.3 us -> 37.3 us (level)
  no operation moved by 1% of the time
where the time goes in v5:
time: 37.3 us; the launch traced here: 37.1 us
  Pallas kernels  34.8 us (93%)
  local copies, waits for them, and re-layouts  2.29 us (6%)
    pallas_call x1, Pallas kernels, body(): pl.pallas_call(functools.partial(kernel, dp_count, pipe_count, lane_width...  34.8 us
    unnamed x1, local copies, waits for them, and re-layouts  2.29 us

profile of v5, /device:TPU:0, one launch (start us, length us, event | category | flops | bytes accessed | tf_op | source)
XLA Modules:
  0.0 37.1 jit_solution(1477332317289260749)
XLA Ops:
  0.0 34.8 %shard_map.46 = bf16[1,1,128,4096]{3,2,1,0:T(8,128)(2,1)} custom-call(bf16[1,1,128,4096]{3,2,1,0:T(8,128)(2,1)} %gate.1, bf16[16,128]{1,0:T(8,128)(2,1)} %bitcast.1, s32[1,128]{1,0:T(1,128)} %docs_hbm.1, bf16[1,128,4096]{2,1,0:T(8,128)(2,1)} %loss.1), custom_call_target="tpu_custom_call" | custom-call | flops 4294967296 | bytes 3145728 | tf_op jit(solution)/shard_map/pallas_call | solution.py:266
  34.8 2.3 %copy.6 = bf16[1,1,128,4096]{3,2,1,0:T(8,128)(2,1)} copy(bf16[1,1,128,4096]{3,2,1,0:T(8,128)(2,1)} %shard_map.46) | data formatting | bytes 2097152

commit v6 on v5

--- a/solution.py
+++ b/solution.py
@@ -9,7 +9,8 @@
 
 MESH_ID = pl.DeviceIdType.MESH
 CHUNK = 256
-LAG = 4
+LAG = 5
+PLANE = 4
 DOT_GROUPS = 4
 
 
@@ -29,6 +30,11 @@
     has_below = stage > 0
     has_before = me > 0
     has_next = me < dp_count - 1
+    planes = dp_count // PLANE
+    plane, place = me // PLANE, lax.rem(me, PLANE)
+    plane_after, plane_before = plane < planes - 1, plane > 0
+    next_apart = jnp.logical_and(place == PLANE - 1, plane_after)
+    before_apart = jnp.logical_and(place == 0, plane_before)
 
     def columns(j):
         return pl.ds(pl.multiple_of(j * width, width), width)
@@ -42,11 +48,33 @@
     def out_copy(j):
         return pltpu.make_async_copy(obuf.at[j], out.at[0, 0, :, columns(j)], osem.at[j])
 
-    def filter_copy(slot, peer):
+    def filter_copy(slot, peer, way):
         return pltpu.make_async_remote_copy(
-            src_ref=filt, dst_ref=fall.at[slot], send_sem=fsend.at[peer], recv_sem=frecv.at[slot],
+            src_ref=fall.at[slot], dst_ref=fall.at[slot],
+            send_sem=fsend.at[slot // PLANE, way], recv_sem=frecv.at[slot],
             device_id=(stage, peer), device_id_type=MESH_ID,
         )
+
+    def beside(k):
+        return plane * PLANE + lax.rem(place + k, PLANE)
+
+    def each_forward(p, act):
+        slot = p * PLANE + place
+
+        @pl.when(jnp.logical_and(p <= plane, plane_after))
+        def _():
+            act(filter_copy(slot, me + PLANE, 0))
+
+        @pl.when(jnp.logical_and(p >= plane, plane_before))
+        def _():
+            act(filter_copy(slot, me - PLANE, 1))
+
+        for k in range(1, PLANE):
+            act(filter_copy(slot, beside(k), 1 + k))
+
+    def forward(p):
+        filter_copy(p * PLANE + place, beside(1), 0).wait_recv()
+        each_forward(p, lambda copy: copy.start())
 
     def halo_copy(j):
         return pltpu.make_async_remote_copy(
@@ -84,12 +112,17 @@
 
     barrier = pltpu.get_barrier_semaphore()
 
-    def greet(k):
-        pl.semaphore_signal(
-            barrier, inc=1, device_id=(stage, lax.rem(me + k + 1, dp_count)), device_id_type=MESH_ID
-        )
-
-    each(dp_count - 1, greet)
+    def greet(peer):
+        pl.semaphore_signal(barrier, inc=1, device_id=(stage, peer), device_id_type=MESH_ID)
+
+    for k in range(1, PLANE):
+        greet(beside(k))
+    for near, step_by in (
+        (plane_after, PLANE), (plane_before, -PLANE), (next_apart, 1), (before_apart, -1)
+    ):
+        @pl.when(near)
+        def _(step_by=step_by):
+            greet(me + step_by)
 
     @pl.when(has_below)
     def _():
@@ -104,18 +137,16 @@
     docs_own[...] = jnp.broadcast_to(docs[...], docs_own.shape)
     fall[me] = filt[...]
 
-    greeted = dp_count - 1 + has_below.astype(jnp.int32) + not_last_stage.astype(jnp.int32)
+    greeted = PLANE - 1
+    for near in (plane_after, plane_before, next_apart, before_apart, has_below, not_last_stage):
+        greeted = greeted + near.astype(jnp.int32)
     pl.semaphore_wait(barrier, greeted)
 
-    def send_filters(k):
-        peer = lax.rem(me + k + 1, dp_count)
-        filter_copy(me, peer).start()
-
     @pl.when(has_before)
     def _():
         docs_copy().start()
 
-    each(dp_count - 1, send_filters)
+    each_forward(plane, lambda copy: copy.start())
 
     def scale(j):
         gate_copy(j).wait()
@@ -174,9 +205,9 @@
         for q in range(slots):
             slot = j * slots + q
 
-            @pl.when(slot != me)
+            @pl.when(lax.rem(slot, PLANE) != place)
             def _():
-                filter_copy(slot, slot).wait_recv()
+                filter_copy(slot, beside(1), 0).wait_recv()
 
 
     def produce(j):
@@ -220,7 +251,21 @@
 
     lag = LAG * not_last_stage.astype(jnp.int32)
 
+    @pl.when(plane_before)
+    def _():
+        forward(0)
+
+    plane_steps = PLANE // slots
+
     def step(s):
+        upcoming = s // plane_steps + 1
+
+        @pl.when(jnp.logical_and(
+            jnp.logical_and(lax.rem(s, plane_steps) == 0, upcoming < planes), upcoming != plane
+        ))
+        def _():
+            forward(upcoming)
+
         @pl.when(jnp.logical_and(not_last_stage, s < chunk_count))
         def _():
             scale(s)
@@ -248,7 +293,7 @@
     def _():
         docs_copy().wait_send()
 
-    each(dp_count - 1, lambda k: filter_copy(me, lax.rem(me + k + 1, dp_count)).wait_send())
+    each(planes, lambda p: each_forward(p, lambda copy: copy.wait_send()))
 
 
 def body(mesh_shape, gate, filters, doc_ids, loss_grad):
@@ -284,7 +329,7 @@
             pltpu.VMEM((rows, rows), jnp.bfloat16),
             pltpu.VMEM((rows, rows), jnp.bfloat16),
             dma((chunk_count,)), dma((chunk_count,)), dma((chunk_count,)),
-            dma((dp_count,)), dma((dp_count,)),
+            dma((dp_count // PLANE, PLANE + 1)), dma((dp_count,)),
             dma((chunk_count,)), dma((chunk_count,)),
             dma((chunk_count,)), dma((chunk_count,)),
             dma, dma,

time: 37.3 us -> 45.1 us (1.21)
  Pallas kernels: 34.8 us -> 42.6 us
    pallas_call x1, Pallas kernels: 34.8 us -> 42.6 us  [body(): pl.pallas_call(functools.partial(kernel, dp_count, pipe_count, lane_width...]
where the time goes in v6:
time: 45.1 us; the launch traced here: 44.9 us
  Pallas kernels  42.6 us (94%)
  local copies, waits for them, and re-layouts  2.29 us (5%)
    pallas_call x1, Pallas kernels, body(): pl.pallas_call(functools.partial(kernel, dp_count, pipe_count, lane_width...  42.6 us
    unnamed x1, local copies, waits for them, and re-layouts  2.29 us

profile of v6, /device:TPU:0, one launch (start us, length us, event | category | flops | bytes accessed | tf_op | source)
XLA Modules:
  0.0 44.9 jit_solution(8374977786687115501)
XLA Ops:
  0.0 42.6 %shard_map.46 = bf16[1,1,128,4096]{3,2,1,0:T(8,128)(2,1)} custom-call(bf16[1,1,128,4096]{3,2,1,0:T(8,128)(2,1)} %gate.1, bf16[16,128]{1,0:T(8,128)(2,1)} %bitcast.1, s32[1,128]{1,0:T(1,128)} %docs_hbm.1, bf16[1,128,4096]{2,1,0:T(8,128)(2,1)} %loss.1), custom_call_target="tpu_custom_call" | custom-call | flops 4294967296 | bytes 3145728 | tf_op jit(solution)/shard_map/pallas_call | solution.py:311
  42.6 2.3 %copy.6 = bf16[1,1,128,4096]{3,2,1,0:T(8,128)(2,1)} copy(bf16[1,1,128,4096]{3,2,1,0:T(8,128)(2,1)} %shard_map.46) | data formatting | bytes 2097152

commit v7 on v5

--- a/solution.py
+++ b/solution.py
@@ -10,6 +10,7 @@
 MESH_ID = pl.DeviceIdType.MESH
 CHUNK = 256
 LAG = 4
+AHEAD = 5
 DOT_GROUPS = 4
 
 
@@ -139,7 +140,7 @@
 
     @pl.when(is_last_stage)
     def _():
-        each(chunk_count, scale)
+        each(AHEAD, scale)
 
     @pl.when(jnp.logical_not(has_next))
     def _():
@@ -221,6 +222,10 @@
     lag = LAG * not_last_stage.astype(jnp.int32)
 
     def step(s):
+        @pl.when(jnp.logical_and(is_last_stage, s + AHEAD < chunk_count))
+        def _():
+            scale(s + AHEAD)
+
         @pl.when(jnp.logical_and(not_last_stage, s < chunk_count))
         def _():
             scale(s)

time: 37.3 us -> 37.3 us (level)
  no operation moved by 1% of the time
where the time goes in v7:
time: 37.3 us; the launch traced here: 37.1 us
  Pallas kernels  34.8 us (93%)
  local copies, waits for them, and re-layouts  2.29 us (6%)
    pallas_call x1, Pallas kernels, body(): pl.pallas_call(functools.partial(kernel, dp_count, pipe_count, lane_width...  34.8 us
    unnamed x1, local copies, waits for them, and re-layouts  2.29 us

profile of v7, /device:TPU:0, one launch (start us, length us, event | category | flops | bytes accessed | tf_op | source)
XLA Modules:
  0.0 37.1 jit_solution(17263172826201316433)
XLA Ops:
  0.0 34.8 %shard_map.46 = bf16[1,1,128,4096]{3,2,1,0:T(8,128)(2,1)} custom-call(bf16[1,1,128,4096]{3,2,1,0:T(8,128)(2,1)} %gate.1, bf16[16,128]{1,0:T(8,128)(2,1)} %bitcast.1, s32[1,128]{1,0:T(1,128)} %docs_hbm.1, bf16[1,128,4096]{2,1,0:T(8,128)(2,1)} %loss.1), custom_call_target="tpu_custom_call" | custom-call | flops 4294967296 | bytes 3145728 | tf_op jit(solution)/shard_map/pallas_call | solution.py:271
  34.8 2.3 %copy.6 = bf16[1,1,128,4096]{3,2,1,0:T(8,128)(2,1)} copy(bf16[1,1,128,4096]{3,2,1,0:T(8,128)(2,1)} %shard_map.46) | data formatting | bytes 2097152

commit v8 on v7

--- a/solution.py
+++ b/solution.py
@@ -9,8 +9,8 @@
 
 MESH_ID = pl.DeviceIdType.MESH
 CHUNK = 256
-LAG = 4
-AHEAD = 5
+LAG = 2
+AHEAD = 3
 DOT_GROUPS = 4
 
 

time: 37.3 us -> 41.8 us (1.12)
  Pallas kernels: 34.8 us -> 39.4 us
    pallas_call x1, Pallas kernels: 34.8 us -> 39.4 us  [body(): pl.pallas_call(functools.partial(kernel, dp_count, pipe_count, lane_width...]
where the time goes in v8:
time: 41.8 us; the launch traced here: 41.7 us
  Pallas kernels  39.4 us (94%)
  local copies, waits for them, and re-layouts  2.29 us (5%)
    pallas_call x1, Pallas kernels, body(): pl.pallas_call(functools.partial(kernel, dp_count, pipe_count, lane_width...  39.4 us
    unnamed x1, local copies, waits for them, and re-layouts  2.29 us

profile of v8, /device:TPU:0, one launch (start us, length us, event | category | flops | bytes accessed | tf_op | source)
XLA Modules:
  0.0 41.7 jit_solution(11366572873220013115)
XLA Ops:
  0.0 39.4 %shard_map.46 = bf16[1,1,128,4096]{3,2,1,0:T(8,128)(2,1)} custom-call(bf16[1,1,128,4096]{3,2,1,0:T(8,128)(2,1)} %gate.1, bf16[16,128]{1,0:T(8,128)(2,1)} %bitcast.1, s32[1,128]{1,0:T(1,128)} %docs_hbm.1, bf16[1,128,4096]{2,1,0:T(8,128)(2,1)} %loss.1), custom_call_target="tpu_custom_call" | custom-call | flops 4294967296 | bytes 3145728 | tf_op jit(solution)/shard_map/pallas_call | solution.py:271
  39.4 2.3 %copy.6 = bf16[1,1,128,4096]{3,2,1,0:T(8,128)(2,1)} copy(bf16[1,1,128,4096]{3,2,1,0:T(8,128)(2,1)} %shard_map.46) | data formatting | bytes 2097152
